TPU v7x, 32 devices: a whole 2x2x4 slice. The times are simulated.
32 devices in a mesh: dp: 8 (over z, core), tensor: 4 (over y, x).
Axes of the slice: x: 2, y: 2, z: 4, core: 2. Of those that a mesh axis runs over, the one named last changes fastest.
Arguments:
- tokens: bfloat16 [512, 4096], P(('dp', 'tensor')), may hold values from -6 to 6
- norm_gain: float32 [4096], replicated, may hold values from 0.1 to 1.9
- gate_tiles: bfloat16 [4, 8, 256, 4096], P('tensor', 'dp'), may hold values from -0.125 to 0.125
- up_tiles: bfloat16 [4, 8, 256, 4096], P('tensor', 'dp'), may hold values from -0.125 to 0.125
- down_tiles: bfloat16 [4, 8, 256, 4096], P('tensor', 'dp'), may hold values from -0.0625 to 0.0625
- tile_ids: int32 [4, 8, 3, 256], P('tensor', 'dp'), may hold values from 0 to 447, as said below
- tile_counts: int32 [4, 8, 3], P('tensor', 'dp'), may hold values from 128 to 256, as said below
Outputs:
- mixed: bfloat16 [512, 4096], P(('dp', 'tensor'))
Inputs may be any that keep to these rules, and one draw needn't show every extreme that they name: `tile_ids`: each device's slots of one matrix name distinct tiles of its shard; local tile l lies in tile row l // 56 and tile column l % 56 of the shard. `tile_counts`: only the first count slots of a matrix on a device hold kept tiles; for each matrix some device has all 256 slots kept.
All inputs are finite; a program needn't handle non-finite values.
Results may differ from a plain program's by a relative error of at most 0.014.
Values may be sent and summed in bfloat16 or wider, within the bound.
A program may use at most 256 MiB of HBM per device.

v0:
```python
import jax
import jax.numpy as jnp
from jax import lax
from jax.experimental import pallas as pl
from jax.experimental.pallas import tpu as pltpu
from jax.sharding import PartitionSpec as P

D = 4096
FF = 14336
TILE = 64


def normalize(values, norm_gain):
    wide = values.astype(jnp.float32)
    meansq = jnp.mean(wide * wide, axis=-1, keepdims=True)
    return (wide * lax.rsqrt(meansq + 1e-05) * norm_gain).astype(jnp.bfloat16)


def unpack_tiles(packed, slot_ids, counts, row_tiles, col_tiles):
    local_tiles = row_tiles * col_tiles
    slots = slot_ids.shape[0]
    active = jnp.arange(slots) < counts
    select = ((slot_ids[:, None] == jnp.arange(local_tiles)[None, :]) & active[:, None]).astype(
        jnp.bfloat16
    )
    placed = jnp.einsum("kl,ke->le", select, packed, preferred_element_type=jnp.float32).astype(
        jnp.bfloat16
    )
    return placed.reshape(row_tiles, col_tiles, TILE, TILE)


def inward_block(packed, slot_ids, counts, row_tiles, col_tiles):
    placed = unpack_tiles(packed, slot_ids, counts, row_tiles, col_tiles)
    return placed.transpose(0, 2, 1, 3).reshape(row_tiles * TILE, col_tiles * TILE)


def outward_block(packed, slot_ids, counts, row_tiles, col_tiles):
    placed = unpack_tiles(packed, slot_ids, counts, row_tiles, col_tiles)
    return placed.transpose(1, 2, 0, 3).reshape(col_tiles * TILE, row_tiles * TILE)


def even_odd(width):
    source = jnp.arange(width)[:, None]
    place = jnp.arange(width)[None, :]
    inner = place % TILE
    wanted = place - inner + 2 * (inner % (TILE // 2)) + inner // (TILE // 2)
    return (source == wanted).astype(jnp.bfloat16)


def unpack_kernel(row_tiles, col_tiles, outward, ids_ref, packed_ref, out_ref, spread):
    slots = packed_ref.shape[0]
    pairs = TILE // 2
    blocks = col_tiles // 8
    tiles = row_tiles * col_tiles
    wide = 512
    tile = lax.broadcasted_iota(jnp.int32, (tiles, slots), 0)
    select = (tile == ids_ref[...]).astype(jnp.bfloat16)

    def place(step, carry):
        columns = pl.ds(pl.multiple_of(step * wide, wide), wide)
        placed = jnp.dot(select, packed_ref[:, columns], preferred_element_type=jnp.float32)
        for sub in range(wide // 128):
            for block in range(tiles // 8):
                start = block * pairs * 8 + (step * (wide // 128) + sub) * 8
                spread[pl.ds(pl.multiple_of(start, 8), 8), :] = placed[
                    block * 8 : block * 8 + 8, sub * 128 : sub * 128 + 128
                ]
        return carry

    lax.fori_loop(0, TILE * TILE // wide, place, 0)
    low = lax.broadcasted_iota(jnp.int32, (pairs, 128), 1) < TILE

    def join(left, right):
        even = jnp.where(low, left, pltpu.roll(right, TILE, 1))
        odd = jnp.where(low, pltpu.roll(left, TILE, 1), right)
        return even.astype(jnp.bfloat16), odd.astype(jnp.bfloat16)

    def build(step, carry):
        def tile_at(row, sub):
            start = (row * blocks + step // 2) * pairs * 8 + (step % 2) * 4 + sub
            return spread[pl.ds(start, pairs, stride=8), :]

        if outward:
            for sub in range(4):
                for half in range(row_tiles // 2):
                    parts = join(tile_at(2 * half, sub), tile_at(2 * half + 1, sub))
                    for odd in range(2):
                        at = sub * TILE + odd * pairs
                        out_ref[step, at : at + pairs, half * 128 : half * 128 + 128] = parts[odd]
        else:
            for row in range(row_tiles):
                for half in range(2):
                    parts = join(tile_at(row, 2 * half), tile_at(row, 2 * half + 1))
                    for odd in range(2):
                        at = row * TILE + odd * pairs
                        out_ref[step, at : at + pairs, half * 128 : half * 128 + 128] = parts[odd]
        return carry

    lax.fori_loop(0, col_tiles // 4, build, 0)


def unpack(packed, ids, row_tiles, col_tiles, outward):
    groups = col_tiles // 4
    if outward:
        shape = (groups, 4 * TILE, row_tiles * TILE)
    else:
        shape = (groups, row_tiles * TILE, 4 * TILE)
    return pl.pallas_call(
        lambda *refs: unpack_kernel(row_tiles, col_tiles, outward, *refs),
        out_shape=jax.ShapeDtypeStruct(shape, jnp.bfloat16),
        in_specs=[pl.BlockSpec(memory_space=pltpu.VMEM)] * 2,
        out_specs=pl.BlockSpec(memory_space=pltpu.VMEM),
        scratch_shapes=[pltpu.VMEM((row_tiles * col_tiles * TILE // 2, 128), jnp.float32)],
        compiler_params=pltpu.CompilerParams(vmem_limit_bytes=32 << 20),
        cost_estimate=pl.CostEstimate(flops=2 * 10**9, bytes_accessed=6 << 20, transcendentals=0),
        name="unpack_out" if outward else "unpack_in",
    )(ids, packed)


def gather_features(tokens, norm_gain):
    n_dp = lax.axis_size("dp")
    rows = tokens.shape[0]
    normed = normalize(tokens, norm_gain)
    mine = lax.all_to_all(
        normed.reshape(rows, n_dp, D // n_dp).transpose(1, 0, 2), "dp", 0, 0, tiled=True
    )
    mine = lax.all_gather(mine, "tensor", axis=1, tiled=True)
    return mine.reshape(n_dp * lax.axis_size("tensor") * rows, D // n_dp)


def spread_rows(part):
    part = lax.all_to_all(part.astype(jnp.bfloat16), "dp", 0, 1, tiled=True)
    return lax.psum_scatter(part, "tensor", scatter_dimension=0, tiled=True)


def swiglu(gate, upward):
    gate = gate.astype(jnp.float32)
    return (jax.nn.silu(gate) * upward.astype(jnp.float32)).astype(jnp.bfloat16)


def local_plain(tokens, norm_gain, gate_tiles, up_tiles, down_tiles, tile_ids, tile_counts):
    row_tiles = D // (TILE * lax.axis_size("dp"))
    col_tiles = FF // (TILE * lax.axis_size("tensor"))
    ids, counts = tile_ids[0, 0], tile_counts[0, 0]
    mine = gather_features(tokens, norm_gain)
    gate_block = inward_block(gate_tiles[0, 0], ids[0], counts[0], row_tiles, col_tiles)
    up_block = inward_block(up_tiles[0, 0], ids[1], counts[1], row_tiles, col_tiles)
    down_block = outward_block(down_tiles[0, 0], ids[2], counts[2], row_tiles, col_tiles)
    gate = jnp.dot(mine, gate_block, preferred_element_type=jnp.float32)
    gate = lax.psum_scatter(gate, "dp", scatter_dimension=0, tiled=True)
    upward = jnp.dot(mine, up_block, preferred_element_type=jnp.float32)
    upward = lax.psum_scatter(upward, "dp", scatter_dimension=0, tiled=True)
    hidden = lax.all_gather(swiglu(gate, upward), "dp", axis=0, tiled=True)
    return spread_rows(jnp.dot(hidden, down_block, preferred_element_type=jnp.float32))


def local(tokens, norm_gain, gate_tiles, up_tiles, down_tiles, tile_ids, tile_counts):
    n_dp = lax.axis_size("dp")
    row_tiles = D // (TILE * n_dp)
    col_tiles = FF // (TILE * lax.axis_size("tensor"))
    if col_tiles % 8 != 0 or row_tiles % 4 != 0:
        return local_plain(
            tokens, norm_gain, gate_tiles, up_tiles, down_tiles, tile_ids, tile_counts
        )
    slots = tile_ids.shape[-1]
    kept = jnp.arange(slots)[None, :] < tile_counts[0, 0][:, None]
    ids = jnp.where(kept, tile_ids[0, 0], -1)
    mine = gather_features(tokens, norm_gain)
    order = even_odd(256)
    mine = jnp.concatenate(
        [jnp.dot(mine[:, at : at + 256], order) for at in range(0, mine.shape[1], 256)], axis=1
    )
    gate_block = unpack(gate_tiles[0, 0], ids[0:1], row_tiles, col_tiles, False)
    up_block = unpack(up_tiles[0, 0], ids[1:2], row_tiles, col_tiles, False)
    down_block = unpack(down_tiles[0, 0], ids[2:3], row_tiles, col_tiles, True)

    def project(block):
        part = jnp.einsum("tk,gkn->gtn", mine, block, preferred_element_type=jnp.float32)
        return lax.psum_scatter(part.astype(jnp.bfloat16), "dp", scatter_dimension=1, tiled=True)

    hidden = swiglu(project(gate_block), project(up_block))
    hidden = jnp.einsum("gtn,nm->gtm", hidden, order, preferred_element_type=jnp.float32)
    hidden = lax.all_gather(hidden.astype(jnp.bfloat16), "dp", axis=1, tiled=True)
    part = jnp.einsum("gtn,gnf->tf", hidden, down_block, preferred_element_type=jnp.float32)
    return spread_rows(part)


def solution(mesh):
    return jax.shard_map(
        local,
        mesh=mesh,
        in_specs=(
            P(("dp", "tensor"), None),
            P(),
            P("tensor", "dp", None, None),
            P("tensor", "dp", None, None),
            P("tensor", "dp", None, None),
            P("tensor", "dp", None, None),
            P("tensor", "dp", None),
        ),
        out_specs=P(("dp", "tensor"), None),
        check_vma=False,
    )
```

profile of v0, /device:TPU:0, one launch (start us, length us, event | category | flops | bytes accessed | tf_op | source)
XLA Modules:
  0.0 248.2 jit_solution(7771454262538258601)
XLA Ops:
  6.5 1.0 fusion.7
  7.6 1.0 fusion.9
  8.7 0.7 copy.21
  9.4 6.3 %all-to-all-start = ((bf16[8,16,512]{2,1,0:T(8,128)(2,1)}), bf16[8,16,512]{2,1,0:T(8,128)(2,1)S(1)}, u32[]{:S(2)}, u32[]{:S(2)}) async-start(bf16[8,16,512]{2,1,0:T(8,128)(2,1)} %copy.21), calls=%async_computation | async-start | bytes 262144 | tf_op jit(solution)/shard_map/all_to_all | solution.py:124
  15.7 0.0 reduce-scatter.4.cloned.1.call-start
  15.7 0.8 bitcast_select_fusion
  16.5 0.0 copy-start
  16.5 1.6 copy-done
  18.1 4.7 %unpack_in.2 = bf16[14,512,256]{2,1,0:T(8,128)(2,1)S(1)} custom-call(s32[1,256]{1,0:T(1,128)S(1)} %get-tuple-element.7.refs_0_, bf16[256,4096]{1,0:T(8,128)(2,1)S(1)} %bitcast.35), custom_call_target="tpu_custom_call" | custom-call | flops 2000000000 | bytes 6291456 | tf_op jit(solution)/shard_map/unpack_in/pallas_call | solution.py:108
  22.8 0.0 copy-start.3
  22.8 1.8 copy-done.3
  24.5 0.0 all-to-all-done
  24.6 0.1 copy.22
  24.6 10.7 %all_gather.6 = bf16[8,64,512]{2,0,1:T(8,128)(2,1)S(1)} all-gather(bf16[8,16,512]{2,0,1:T(8,128)(2,1)S(1)} %copy.22), channel_id=1, replica_groups=mesh['dp'=8,'tensor'=4] {'tensor'}, dimensions={1}, use_global_device_ids=true | all-gather | bytes 655360 | tf_op jit(solution)/shard_map/all_gather | solution.py:127
  35.3 0.2 copy.23
  35.5 0.3 fusion.10
  35.7 0.3 fusion.12
  36.0 5.9 %convert_bitcast_fusion.1 = bf16[14,512,256]{1,2,0:T(8,128)(2,1)} fusion(bf16[14,512,256]{2,1,0:T(8,128)(2,1)} %copy-done.3, bf16[512,256]{0,1:T(8,128)(2,1)S(1)} %fusion.10, bf16[512,256]{0,1:T(8,128)(2,1)S(1)} %fusion.12), kind=kOutput, calls=%fused_computation.1 | convolution fusion | flops 1881931776 | bytes 7864320 | tf_op jit(solution)/shard_map/tk,gkn->gtn/dot_general | solution.py:178
  42.0 7.9 %copy.26 = bf16[14,512,256]{2,0,1:T(8,128)(2,1)} copy(bf16[14,512,256]{1,2,0:T(8,128)(2,1)} %convert_bitcast_fusion.1) | data formatting | bytes 7340032 | tf_op jit(solution)/shard_map/convert_element_type | solution.py:179
  49.9 0.0 copy-start.1
  49.9 0.0 reduce-scatter.4.cloned.1.call-update
  49.9 0.0 reduce-scatter.6.cloned.1.call-start
  50.0 1.5 copy-done.1
  51.5 4.7 %unpack_in.3 = bf16[14,512,256]{2,1,0:T(8,128)(2,1)S(1)} custom-call(s32[1,256]{1,0:T(1,128)S(1)} %get-tuple-element.6.refs_0_, bf16[256,4096]{1,0:T(8,128)(2,1)S(1)} %bitcast.36), custom_call_target="tpu_custom_call" | custom-call | flops 2000000000 | bytes 6291456 | tf_op jit(solution)/shard_map/unpack_in/pallas_call | solution.py:108
  56.2 3.9 %convert_bitcast_fusion = bf16[14,512,256]{1,2,0:T(8,128)(2,1)} fusion(bf16[14,512,256]{2,1,0:T(8,128)(2,1)S(1)} %unpack_in.3, bf16[512,256]{0,1:T(8,128)(2,1)S(1)} %fusion.10, bf16[512,256]{0,1:T(8,128)(2,1)S(1)} %fusion.12), kind=kOutput, calls=%fused_computation | convolution fusion | flops 1881931776 | bytes 7864320 | tf_op jit(solution)/shard_map/tk,gkn->gtn/dot_general | solution.py:178
  60.1 8.0 %copy.29 = bf16[14,512,256]{2,0,1:T(8,128)(2,1)} copy(bf16[14,512,256]{1,2,0:T(8,128)(2,1)} %convert_bitcast_fusion) | data formatting | bytes 7340032 | tf_op jit(solution)/shard_map/convert_element_type | solution.py:179
  68.1 0.0 copy-start.2
  68.1 0.0 reduce-scatter.6.cloned.1.call-update
  68.1 0.0 all-gather.2.cloned.1.call-start
  68.2 31.8 %reduce-scatter.4.cloned.1.call-done = bf16[14,64,256]{2,0,1:T(8,128)(2,1)} async-done(((bf16[14,512,256]{2,0,1:T(8,128)(2,1)}), bf16[14,64,256]{2,0,1:T(8,128)(2,1)}) %reduce-scatter.4.cloned.1.call-update) | async-done | bytes 458768 | tf_op jit(solution)/shard_map/reduce_scatter | solution.py:179
  100.0 50.5 %reduce-scatter.6.cloned.1.call-done = bf16[14,64,256]{2,0,1:T(8,128)(2,1)} async-done(((bf16[14,512,256]{2,0,1:T(8,128)(2,1)}), bf16[14,64,256]{2,0,1:T(8,128)(2,1)}) %reduce-scatter.6.cloned.1.call-update) | async-done | bytes 458768 | tf_op jit(solution)/shard_map/reduce_scatter | solution.py:179
  150.5 1.5 fusion.5
  152.0 1.1 convolution_convert_fusion
  153.1 0.0 all-gather.2.cloned.1.call-update
  153.1 0.0 reduce-scatter.8.cloned.1.call-start
  153.2 0.0 copy-done.2
  153.2 5.1 %unpack_out.1 = bf16[14,256,512]{2,1,0:T(8,128)(2,1)S(1)} custom-call(s32[1,256]{1,0:T(1,128)S(1)} %get-tuple-element.5.refs_0_, bf16[256,4096]{1,0:T(8,128)(2,1)S(1)} %bitcast.37), custom_call_target="tpu_custom_call" | custom-call | flops 2000000000 | bytes 6291456 | tf_op jit(solution)/shard_map/unpack_out/pallas_call | solution.py:108
  158.3 0.0 copy-start.4
  158.3 1.8 copy-done.4
  160.1 33.9 %all-gather.2.cloned.1.call-done = bf16[14,512,256]{2,1,0:T(8,128)(2,1)} async-done(((bf16[14,64,256]{2,1,0:T(8,128)(2,1)}), bf16[14,512,256]{2,1,0:T(8,128)(2,1)}) %all-gather.2.cloned.1.call-update) | async-done | bytes 3670032 | tf_op jit(solution)/shard_map/all_gather | solution.py:183
  194.0 5.2 %fusion = bf16[512,512]{1,0:T(8,128)(2,1)S(1)} fusion(bf16[14,512,256]{2,1,0:T(8,128)(2,1)} %all-gather.2.cloned.1.call-done, bf16[14,256,512]{2,1,0:T(8,128)(2,1)} %copy-done.4), kind=kOutput, calls=%fused_computation.5 | convolution fusion | flops 1879310336 | bytes 7864320 | tf_op jit(solution)/shard_map/gtn,gnf->tf/dot_general | solution.py:184
  199.2 17.9 %all_to_all.24 = bf16[8,64,512]{2,1,0:T(8,128)(2,1)S(1)} all-to-all(bf16[8,64,512]{2,1,0:T(8,128)(2,1)S(1)} %bitcast.42), channel_id=1, replica_groups=mesh['dp'=8,'tensor'=4] {'dp'}, dimensions={0} | all-to-all | bytes 1048576 | tf_op jit(solution)/shard_map/all_to_all | solution.py:132
  217.1 0.8 copy.39
  217.9 0.0 reduce-scatter.8.cloned.1.call-update
  217.9 23.7 %reduce-scatter.8.cloned.1.call-done = bf16[16,4096]{1,0:T(8,128)(2,1)} async-done(((bf16[64,4096]{1,0:T(8,128)(2,1)}), bf16[16,4096]{1,0:T(8,128)(2,1)}) %reduce-scatter.8.cloned.1.call-update) | async-done | bytes 131088 | tf_op jit(solution)/shard_map/reduce_scatter | solution.py:133
  (4 shorter events, 0.1 us)
Async XLA Ops:
  9.4 15.2 %all-to-all-start = ((bf16[8,16,512]{2,1,0:T(8,128)(2,1)}), bf16[8,16,512]{2,1,0:T(8,128)(2,1)S(1)}, u32[]{:S(2)}, u32[]{:S(2)}) async-start(bf16[8,16,512]{2,1,0:T(8,128)(2,1)} %copy.21), calls=%async_computation | async-start | bytes 262144 | tf_op jit(solution)/shard_map/all_to_all | solution.py:124
  15.7 84.3 %reduce-scatter.4.cloned.1.call-start = ((), (), s32[]{:S(2)}) async-start(), calls=%async_computation.5 | async-start | bytes 4718592 | tf_op jit(solution)/shard_map/reduce_scatter | solution.py:179
  16.5 1.6 copy-start
  22.8 1.8 copy-start.3
  49.9 1.6 copy-start.1
  49.9 100.5 %reduce-scatter.6.cloned.1.call-start = ((), (), s32[]{:S(2)}) async-start(), calls=%async_computation.6 | async-start | bytes 4718592 | tf_op jit(solution)/shard_map/reduce_scatter | solution.py:179
  68.1 85.0 %copy-start.2 = (bf16[1,1,256,4096]{3,2,1,0:T(8,128)(2,1)S(1)}, bf16[1,1,256,4096]{3,2,1,0:T(8,128)(2,1)}, u32[]{:S(2)}) copy-start(bf16[1,1,256,4096]{3,2,1,0:T(8,128)(2,1)} %param.11) | copy-start | bytes 6291460
  68.1 125.8 %all-gather.2.cloned.1.call-start = ((), (), s32[]{:S(2)}) async-start(), calls=%async_computation.7 | async-start | bytes 4128768 | tf_op jit(solution)/shard_map/all_gather | solution.py:183
  153.1 88.5 %reduce-scatter.8.cloned.1.call-start = ((), (), s32[]{:S(2)}) async-start(), calls=%async_computation.8 | async-start | bytes 655360 | tf_op jit(solution)/shard_map/reduce_scatter | solution.py:133
  158.3 1.8 copy-start.4
Sparse Core Ops, SparseCore 0:
  50.0 49.8 reduce-scatter.3
  102.3 48.1 reduce-scatter.5
  153.2 40.7 all-gather.1
  218.0 23.5 reduce-scatter.7
where the time goes:
time: 249 us; the launch traced here: 248 us
  waiting for transfers between devices  140 us (56%)
  blocking collectives  28.5 us (11%)
  local copies, waits for them, and re-layouts  24.4 us (10%)
  matrix products  16.7 us (7%)
  Pallas kernels  14.5 us (6%)
  between operations  13.2 us (5%)
  starting transfers between devices  6.49 us (3%)
  other arithmetic  4.35 us (2%)
    reduce_scatter x2, waiting for transfers between devices, project(): lax.psum_scatter(part.astype(jnp.bfloat16), 'dp', scatter_dimension=1, ti...  82.3 us
    all_gather x1, waiting for transfers between devices, local(): lax.all_gather(hidden.astype(jnp.bfloat16), 'dp', axis=1, tiled=True)  33.9 us
    reduce_scatter x1, waiting for transfers between devices, spread_rows(): return lax.psum_scatter(part, 'tensor', scatter_dimension=0, tiled=True)  23.7 us
    all_to_all x1, blocking collectives, spread_rows(): part = lax.all_to_all(part.astype(jnp.bfloat16), 'dp', 0, 1, tiled=True)  17.9 us
    convert_element_type x2, local copies, waits for them, and re-layouts, project(): part.astype(jnp.bfloat16)  15.9 us
    pallas_call x3, Pallas kernels, unpack(): pl.pallas_call(lambda *refs: unpack_kernel(row_tiles, col_tiles, outward,...  14.5 us
    all_gather x1, blocking collectives, gather_features(): mine = lax.all_gather(mine, 'tensor', axis=1, tiled=True)  10.7 us
    dot_general x2, matrix products, project(): jnp.einsum('tk,gkn->gtn', mine, block, preferred_element_type=jnp.float32)  9.89 us
  transfers between devices with their start and end apart: 5, of which 4 were waited for; matrix products, arithmetic and copies ran while one was open for 5% of the time, Pallas kernels for 6%

commit v1 on v0

--- a/solution.py
+++ b/solution.py
@@ -8,6 +8,7 @@
 D = 4096
 FF = 14336
 TILE = 64
+MESH = pl.DeviceIdType.MESH
 
 
 def normalize(values, norm_gain):
@@ -154,35 +155,285 @@
     return spread_rows(jnp.dot(hidden, down_block, preferred_element_type=jnp.float32))
 
 
+def flow_kernel(
+    n_dp, n_tensor, normed, order, gate_w, up_w, down_w, out,
+    xa, xg, xp, part, pair, chain, hid, acc, tail, tail_in, mixed, back,
+    head_s, head_r, row_s, row_r, pair_s, pair_r, chain_s, chain_r,
+    hid_s, hid_r, core_s, core_r, tail_s, tail_r, back_s, back_r,
+):
+    me, mt = lax.axis_index("dp"), lax.axis_index("tensor")
+    z, core = me // 2, me % 2
+    chips = n_dp // 2
+    last = chips - 1
+    groups = gate_w.shape[0]
+    rows, width = xa.shape[1], xa.shape[2]
+    other = 1 - core
+    buddy = z * 2 + other
+    hops = ((last - z, z - 1), (z, z + 1))
+
+    barrier = pltpu.get_barrier_semaphore()
+    for d in range(1, n_dp):
+        pl.semaphore_signal(
+            barrier, inc=1, device_id=((me + d) % n_dp, mt), device_id_type=MESH
+        )
+    for d in range(1, n_tensor):
+        pl.semaphore_signal(
+            barrier, inc=1, device_id=(me, (mt + d) % n_tensor), device_id_type=MESH
+        )
+    pl.semaphore_wait(barrier, n_dp + n_tensor - 2)
+
+    def send(src, dst, send_sem, recv_sem, dp, tensor):
+        return pltpu.make_async_remote_copy(
+            src_ref=src, dst_ref=dst, send_sem=send_sem, recv_sem=recv_sem,
+            device_id=(dp, tensor), device_id_type=MESH,
+        )
+
+    def slab(index):
+        return pl.ds(pl.multiple_of(index * width, width), width)
+
+    def head(d):
+        to = (me + d) % n_dp
+        return send(normed.at[:, slab(to)], xa.at[me], head_s.at[d], head_r.at[d], to, mt)
+
+    def row(d):
+        return send(xa, xg.at[mt], row_s.at[d], row_r.at[d], me, (mt + d) % n_tensor)
+
+    for d in range(1, n_dp):
+        head(d).start()
+    xa[me] = normed[:, slab(me)]
+    for d in range(1, n_dp):
+        head(d).wait_recv()
+    for d in range(1, n_tensor):
+        row(d).start()
+    xg[mt] = xa[...]
+    for d in range(1, n_tensor):
+        row(d).wait_recv()
+    tokens = n_tensor * n_dp * rows
+    quarter = tokens // 4
+    for at in range(0, width, 256):
+        xp[:, at : at + 256] = jnp.dot(
+            xg[:, :, :, at : at + 256].reshape(tokens, 256),
+            order[...],
+            preferred_element_type=jnp.float32,
+        ).astype(jnp.bfloat16)
+    acc[...] = jnp.zeros_like(acc)
+
+    def pair_copy(n):
+        return send(part.at[n, :, other], pair.at[n], pair_s.at[n], pair_r.at[n], buddy, mt)
+
+    def chain_copy(n, h):
+        return send(
+            part.at[n, h, core], chain.at[n, h], chain_s.at[n, h], chain_r.at[n, h],
+            jnp.clip(hops[h][1], 0, last) * 2 + core, mt,
+        )
+
+    def hid_copy(n, h):
+        to = jnp.clip(hops[1 - h][1], 0, last) * 2 + core
+        return send(
+            hid.at[n, h, core], hid.at[n, h, core], hid_s.at[n, h], hid_r.at[n, h], to, mt
+        )
+
+    def core_copy(n, h):
+        return send(
+            hid.at[n, h, core], hid.at[n, h, core], core_s.at[n, h], core_r.at[n, h], buddy, mt
+        )
+
+    def project(n):
+        for which, weight in enumerate((gate_w, up_w)):
+            value = jnp.dot(xp[...], weight[n], preferred_element_type=jnp.float32)
+            part[n, :, :, :, which * 256 : which * 256 + 256] = value.astype(
+                jnp.bfloat16
+            ).reshape(2, 2, quarter, 256)
+        pair_copy(n).start()
+
+    def inside(n):
+        return (n >= 0) & (n < groups)
+
+    ahead = 2
+    for n in range(ahead):
+        project(jnp.int32(n))
+    nearest = jnp.minimum(z, last - z)
+    farthest = jnp.maximum(z, last - z)
+
+    def step(s, carry):
+        @pl.when(inside(s - nearest))
+        def _():
+            pair_copy(s - nearest).wait_recv()
+
+        for h in range(2):
+            position = hops[h][0]
+            n = s - position
+
+            @pl.when(inside(n))
+            def _():
+                def own():
+                    return part[n, h, core].astype(jnp.float32) + pair[n, h].astype(jnp.float32)
+
+                @pl.when(position > 0)
+                def _():
+                    chain_copy(n, h).wait_recv()
+
+                @pl.when(position == 0)
+                def _():
+                    part[n, h, core] = own().astype(jnp.bfloat16)
+
+                @pl.when((position > 0) & (position < last))
+                def _():
+                    part[n, h, core] = (own() + chain[n, h].astype(jnp.float32)).astype(jnp.bfloat16)
+
+                @pl.when(position < last)
+                def _():
+                    chain_copy(n, h).start()
+
+                @pl.when(position == last)
+                def _():
+                    total = own() + chain[n, h].astype(jnp.float32)
+                    gate = total[:, :256]
+                    value = gate / (1.0 + jnp.exp(-gate)) * total[:, 256:]
+                    hid[n, h, core] = jnp.dot(
+                        value.astype(jnp.bfloat16), order[...], preferred_element_type=jnp.float32
+                    ).astype(jnp.bfloat16)
+
+        for h in range(2):
+            distance = last - hops[h][0]
+            n = s - last - distance
+
+            @pl.when(inside(n))
+            def _():
+                @pl.when(distance > 0)
+                def _():
+                    hid_copy(n, h).wait_recv()
+
+                @pl.when(distance < last)
+                def _():
+                    hid_copy(n, h).start()
+
+                core_copy(n, h).start()
+
+        @pl.when(s + ahead < groups)
+        def _():
+            project(s + ahead)
+
+        done = s - last - farthest - 1
+
+        @pl.when(inside(done))
+        def _():
+            for h in range(2):
+                core_copy(done, h).wait_recv()
+            acc[...] += jnp.dot(
+                hid[done].reshape(tokens, 256), down_w[done], preferred_element_type=jnp.float32
+            )
+
+        return carry
+
+    lax.fori_loop(0, groups + 2 * last + 1, step, 0)
+
+    tail[...] = acc[...].astype(jnp.bfloat16).reshape(tail.shape)
+
+    def tail_copy(d):
+        to = (mt + d) % n_tensor
+        return send(tail.at[to], tail_in.at[mt], tail_s.at[d], tail_r.at[d], me, to)
+
+    def back_copy(d):
+        to = (me + d) % n_dp
+        return send(mixed.at[to], back.at[me], back_s.at[d], back_r.at[d], to, mt)
+
+    for d in range(1, n_tensor):
+        tail_copy(d).start()
+    tail_in[mt] = tail[mt]
+    for d in range(1, n_tensor):
+        tail_copy(d).wait_recv()
+    total = tail_in[0].astype(jnp.float32)
+    for t in range(1, n_tensor):
+        total += tail_in[t].astype(jnp.float32)
+    mixed[...] = total.astype(jnp.bfloat16).reshape(mixed.shape)
+    for d in range(1, n_dp):
+        back_copy(d).start()
+    back[me] = mixed[me]
+
+    def drain(n, carry):
+        pair_copy(n).wait_send()
+        for h in range(2):
+            core_copy(n, h).wait_send()
+
+            @pl.when(hops[h][0] < last)
+            def _():
+                chain_copy(n, h).wait_send()
+
+            @pl.when(last - hops[h][0] < last)
+            def _():
+                hid_copy(n, h).wait_send()
+
+        return carry
+
+    lax.fori_loop(0, groups, drain, 0)
+    for d in range(1, n_dp):
+        head(d).wait_send()
+        back_copy(d).wait_recv()
+        back_copy(d).wait_send()
+    for d in range(1, n_tensor):
+        row(d).wait_send()
+        tail_copy(d).wait_send()
+    for p in range(n_dp):
+        out[:, p * width : p * width + width] = back[p]
+
+
+def flow(normed, order, gate_w, up_w, down_w, n_dp, n_tensor):
+    groups, width, _ = gate_w.shape
+    rows = normed.shape[0]
+    tokens = rows * n_dp * n_tensor
+    quarter = tokens // 4
+    half = jnp.bfloat16
+    dma = pltpu.SemaphoreType.DMA
+    return pl.pallas_call(
+        lambda *refs: flow_kernel(n_dp, n_tensor, *refs),
+        out_shape=jax.ShapeDtypeStruct(normed.shape, half),
+        in_specs=[pl.BlockSpec(memory_space=pltpu.VMEM)] * 5,
+        out_specs=pl.BlockSpec(memory_space=pltpu.VMEM),
+        scratch_shapes=[
+            pltpu.VMEM((n_dp, rows, width), half),
+            pltpu.VMEM((n_tensor, n_dp, rows, width), half),
+            pltpu.VMEM((tokens, width), half),
+            pltpu.VMEM((groups, 2, 2, quarter, 512), half),
+            pltpu.VMEM((groups, 2, quarter, 512), half),
+            pltpu.VMEM((groups, 2, quarter, 512), half),
+            pltpu.VMEM((groups, 2, 2, quarter, 256), half),
+            pltpu.VMEM((tokens, width), jnp.float32),
+            pltpu.VMEM((n_tensor, n_dp * rows, width), half),
+            pltpu.VMEM((n_tensor, n_dp * rows, width), half),
+            pltpu.VMEM((n_dp, rows, width), half),
+            pltpu.VMEM((n_dp, rows, width), half),
+            dma((n_dp,)), dma((n_dp,)), dma((n_tensor,)), dma((n_tensor,)),
+            dma((groups,)), dma((groups,)), dma((groups, 2)), dma((groups, 2)),
+            dma((groups, 2)), dma((groups, 2)), dma((groups, 2)), dma((groups, 2)),
+            dma((n_tensor,)), dma((n_tensor,)), dma((n_dp,)), dma((n_dp,)),
+        ],
+        compiler_params=pltpu.CompilerParams(
+            collective_id=0, has_side_effects=True, vmem_limit_bytes=56 << 20
+        ),
+        cost_estimate=pl.CostEstimate(
+            flops=6 * 10**9, bytes_accessed=12 << 20, transcendentals=10**6
+        ),
+        name="flow",
+    )(normed, order, gate_w, up_w, down_w)
+
+
 def local(tokens, norm_gain, gate_tiles, up_tiles, down_tiles, tile_ids, tile_counts):
-    n_dp = lax.axis_size("dp")
+    n_dp, n_tensor = lax.axis_size("dp"), lax.axis_size("tensor")
     row_tiles = D // (TILE * n_dp)
-    col_tiles = FF // (TILE * lax.axis_size("tensor"))
-    if col_tiles % 8 != 0 or row_tiles % 4 != 0:
+    col_tiles = FF // (TILE * n_tensor)
+    if col_tiles % 8 != 0 or row_tiles % 4 != 0 or n_tensor != 4 or n_dp % 2 != 0:
         return local_plain(
             tokens, norm_gain, gate_tiles, up_tiles, down_tiles, tile_ids, tile_counts
         )
     slots = tile_ids.shape[-1]
     kept = jnp.arange(slots)[None, :] < tile_counts[0, 0][:, None]
     ids = jnp.where(kept, tile_ids[0, 0], -1)
-    mine = gather_features(tokens, norm_gain)
-    order = even_odd(256)
-    mine = jnp.concatenate(
-        [jnp.dot(mine[:, at : at + 256], order) for at in range(0, mine.shape[1], 256)], axis=1
-    )
-    gate_block = unpack(gate_tiles[0, 0], ids[0:1], row_tiles, col_tiles, False)
-    up_block = unpack(up_tiles[0, 0], ids[1:2], row_tiles, col_tiles, False)
-    down_block = unpack(down_tiles[0, 0], ids[2:3], row_tiles, col_tiles, True)
-
-    def project(block):
-        part = jnp.einsum("tk,gkn->gtn", mine, block, preferred_element_type=jnp.float32)
-        return lax.psum_scatter(part.astype(jnp.bfloat16), "dp", scatter_dimension=1, tiled=True)
-
-    hidden = swiglu(project(gate_block), project(up_block))
-    hidden = jnp.einsum("gtn,nm->gtm", hidden, order, preferred_element_type=jnp.float32)
-    hidden = lax.all_gather(hidden.astype(jnp.bfloat16), "dp", axis=1, tiled=True)
-    part = jnp.einsum("gtn,gnf->tf", hidden, down_block, preferred_element_type=jnp.float32)
-    return spread_rows(part)
+    gate_w = unpack(gate_tiles[0, 0], ids[0:1], row_tiles, col_tiles, False)
+    up_w = unpack(up_tiles[0, 0], ids[1:2], row_tiles, col_tiles, False)
+    down_w = unpack(down_tiles[0, 0], ids[2:3], row_tiles, col_tiles, True)
+    normed = normalize(tokens, norm_gain)
+    return flow(normed, even_odd(256), gate_w, up_w, down_w, n_dp, n_tensor)
 
 
 def solution(mesh):

time: 249 us -> 150 us (0.60)
  waiting for transfers between devices: 140 us -> 0 us
  Pallas kernels: 14.5 us -> 137 us
  blocking collectives: 28.5 us -> 0 us
  matrix products: 16.7 us -> 0 us
  local copies, waits for them, and re-layouts: 24.4 us -> 8.7 us
  between operations: 13.2 us -> 0.07 us
  starting transfers between devices: 6.49 us -> 0 us
    pallas_call x0 -> x1, Pallas kernels: none -> 123 us  [flow(): pl.pallas_call(lambda *refs: flow_kernel(n_dp, n_tensor, *refs), out_shap...]
    reduce_scatter x3 -> x0, waiting for transfers between devices: 106 us -> none  [the longest x2 82.3 us: project(): lax.psum_scatter(part.astype(jnp.bfloat16), 'dp', scatter_dimension=1, ti...]
    all_gather x1 -> x0, waiting for transfers between devices: 33.9 us -> none  [local(): lax.all_gather(hidden.astype(jnp.bfloat16), 'dp', axis=1, tiled=True)]
    all_to_all x1 -> x0, blocking collectives: 17.9 us -> none  [spread_rows(): part = lax.all_to_all(part.astype(jnp.bfloat16), 'dp', 0, 1, tiled=True)]
    dot_general x6 -> x0, matrix products: 16.7 us -> none  [the longest x2 9.89 us: project(): jnp.einsum('tk,gkn->gtn', mine, block, preferred_element_type=jnp.float32)]
    convert_element_type x2 -> x0, local copies, waits for them, and re-layouts: 15.9 us -> none  [project(): part.astype(jnp.bfloat16)]
    all_gather x1 -> x0, blocking collectives: 10.7 us -> none  [gather_features(): mine = lax.all_gather(mine, 'tensor', axis=1, tiled=True)]
    all_to_all x1 -> x0, starting transfers between devices: 6.33 us -> none  [gather_features(): lax.all_to_all(normed.reshape(rows, n_dp, D // n_dp).transpose(1, 0, 2),...]
  transfers between devices with their start and end apart: 5 -> 0, of which waited for: 4 -> 0; matrix products, arithmetic and copies ran while one was open for 5% -> 0% of each run, Pallas kernels for 6% -> 0%
where the time goes in v1:
time: 150 us
  Pallas kernels  137 us (91%)
  local copies, waits for them, and re-layouts  8.7 us (6%)
  other arithmetic  4.17 us (3%)
    pallas_call x1, Pallas kernels, flow(): pl.pallas_call(lambda *refs: flow_kernel(n_dp, n_tensor, *refs), out_shap...  123 us
    pallas_call x3, Pallas kernels, unpack(): pl.pallas_call(lambda *refs: unpack_kernel(row_tiles, col_tiles, outward,...  14.4 us
    unnamed x13, local copies, waits for them, and re-layouts  8.7 us

profile of v1, /device:TPU:0, one launch (start us, length us, event | category | flops | bytes accessed | tf_op | source)
XLA Modules:
  0.0 150.2 jit_solution(11864139417346289001)
XLA Ops:
  0.0 1.0 fusion
  1.1 0.8 bitcast_select_fusion
  1.8 0.7 fusion.3.refs_1_
  2.5 1.7 %fusion.2.refs_0_ = bf16[16,4096]{1,0:T(8,128)(2,1)} fusion(bf16[16,4096]{1,0:T(8,128)(2,1)} %param.7, f32[4096]{0:T(1024)} %param.8, f32[16]{0:T(128)S(1)} %add_rsqrt_fusion), kind=kLoop, calls=%fused_computation.4 | loop fusion | flops 262144 | bytes 278592 | tf_op jit(solution)/shard_map/convert_element_type | solution.py:17
  4.2 0.0 copy-start
  4.2 1.6 %copy-done = bf16[1,1,256,4096]{3,2,1,0:T(8,128)(2,1)S(1)} copy-done((bf16[1,1,256,4096]{3,2,1,0:T(8,128)(2,1)S(1)}, bf16[1,1,256,4096]{3,2,1,0:T(8,128)(2,1)}, u32[]{:S(2)}) %copy-start) | copy-done | bytes 2097176
  5.8 0.0 copy-start.1
  5.8 5.1 %unpack_out.1.refs_4_ = bf16[14,256,512]{2,1,0:T(8,128)(2,1)S(1)} custom-call(s32[1,256]{1,0:T(1,128)S(1)} %get-tuple-element.5.refs_0_, bf16[256,4096]{1,0:T(8,128)(2,1)S(1)} %bitcast.6), custom_call_target="tpu_custom_call" | custom-call | flops 2000000000 | bytes 6291456 | tf_op jit(solution)/shard_map/unpack_out/pallas_call | solution.py:109
  10.9 0.0 copy-start.3
  10.9 1.9 %copy-done.3 = bf16[14,256,512]{2,1,0:T(8,128)(2,1)} copy-done((bf16[14,256,512]{2,1,0:T(8,128)(2,1)}, bf16[14,256,512]{2,1,0:T(8,128)(2,1)S(1)}, u32[]{:S(2)}) %copy-start.3) | copy-done | bytes 3670040
  12.8 0.0 copy-done.1
  12.8 0.0 copy-start.2
  12.8 4.7 %unpack_in.3.refs_3_ = bf16[14,512,256]{2,1,0:T(8,128)(2,1)S(1)} custom-call(s32[1,256]{1,0:T(1,128)S(1)} %get-tuple-element.6.refs_0_, bf16[256,4096]{1,0:T(8,128)(2,1)S(1)} %bitcast.7), custom_call_target="tpu_custom_call" | custom-call | flops 2000000000 | bytes 6291456 | tf_op jit(solution)/shard_map/unpack_in/pallas_call | solution.py:109
  17.5 0.0 copy-start.4
  17.5 1.8 %copy-done.4 = bf16[14,512,256]{2,1,0:T(8,128)(2,1)} copy-done((bf16[14,512,256]{2,1,0:T(8,128)(2,1)}, bf16[14,512,256]{2,1,0:T(8,128)(2,1)S(1)}, u32[]{:S(2)}) %copy-start.4) | copy-done | bytes 3670040
  19.3 0.0 copy-done.2
  19.3 4.7 %unpack_in.2.refs_2_ = bf16[14,512,256]{2,1,0:T(8,128)(2,1)S(1)} custom-call(s32[1,256]{1,0:T(1,128)S(1)} %get-tuple-element.7.refs_0_, bf16[256,4096]{1,0:T(8,128)(2,1)S(1)} %bitcast.8), custom_call_target="tpu_custom_call" | custom-call | flops 2000000000 | bytes 6291456 | tf_op jit(solution)/shard_map/unpack_in/pallas_call | solution.py:109
  24.0 0.0 copy-start.5
  24.0 1.8 %copy-done.5 = bf16[14,512,256]{2,1,0:T(8,128)(2,1)} copy-done((bf16[14,512,256]{2,1,0:T(8,128)(2,1)}, bf16[14,512,256]{2,1,0:T(8,128)(2,1)S(1)}, u32[]{:S(2)}) %copy-start.5) | copy-done | bytes 3670040
  25.8 122.8 %flow.1 = bf16[16,4096]{1,0:T(8,128)(2,1)} custom-call(bf16[16,4096]{1,0:T(8,128)(2,1)} %fusion.2.refs_0_, bf16[256,256]{1,0:T(8,128)(2,1)} %fusion.3.refs_1_, bf16[14,512,256]{2,1,0:T(8,128)(2,1)} %copy-done.5, bf16[14,512,256]{2,1,0:T(8,128)(2,1)} %copy-done.4, bf16[14,256,512]{2,1,0:T(8,128)(2,1)} %copy-done.3), custom_call_target="tpu_custom_call" | custom-call | flops 6000000000 | bytes 12582912 | tf_op jit(solution)/shard_map/flow/pallas_call | solution.py:388
  148.6 1.6 %copy.11 = bf16[16,4096]{1,0:T(8,128)(2,1)} copy(bf16[16,4096]{1,0:T(8,128)(2,1)} %flow.1) | data formatting | bytes 262144
  (3 shorter events, 0.0 us)
Async XLA Ops:
  4.2 1.6 %copy-start = (bf16[1,1,256,4096]{3,2,1,0:T(8,128)(2,1)S(1)}, bf16[1,1,256,4096]{3,2,1,0:T(8,128)(2,1)}, u32[]{:S(2)}) copy-start(bf16[1,1,256,4096]{3,2,1,0:T(8,128)(2,1)} %param.11) | copy-start | bytes 6291460
  5.8 7.0 %copy-start.1 = (bf16[1,1,256,4096]{3,2,1,0:T(8,128)(2,1)S(1)}, bf16[1,1,256,4096]{3,2,1,0:T(8,128)(2,1)}, u32[]{:S(2)}) copy-start(bf16[1,1,256,4096]{3,2,1,0:T(8,128)(2,1)} %param.10) | copy-start | bytes 6291460
  10.9 1.9 %copy-start.3 = (bf16[14,256,512]{2,1,0:T(8,128)(2,1)}, bf16[14,256,512]{2,1,0:T(8,128)(2,1)S(1)}, u32[]{:S(2)}) copy-start(bf16[14,256,512]{2,1,0:T(8,128)(2,1)S(1)} %unpack_out.1.refs_4_) | copy-start | bytes 11010052
  12.8 6.5 %copy-start.2 = (bf16[1,1,256,4096]{3,2,1,0:T(8,128)(2,1)S(1)}, bf16[1,1,256,4096]{3,2,1,0:T(8,128)(2,1)}, u32[]{:S(2)}) copy-start(bf16[1,1,256,4096]{3,2,1,0:T(8,128)(2,1)} %param.9) | copy-start | bytes 6291460
  17.5 1.8 %copy-start.4 = (bf16[14,512,256]{2,1,0:T(8,128)(2,1)}, bf16[14,512,256]{2,1,0:T(8,128)(2,1)S(1)}, u32[]{:S(2)}) copy-start(bf16[14,512,256]{2,1,0:T(8,128)(2,1)S(1)} %unpack_in.3.refs_3_) | copy-start | bytes 11010052
  24.0 1.8 %copy-start.5 = (bf16[14,512,256]{2,1,0:T(8,128)(2,1)}, bf16[14,512,256]{2,1,0:T(8,128)(2,1)S(1)}, u32[]{:S(2)}) copy-start(bf16[14,512,256]{2,1,0:T(8,128)(2,1)S(1)} %unpack_in.2.refs_2_) | copy-start | bytes 11010052

commit v2 on v1

--- a/solution.py
+++ b/solution.py
@@ -38,84 +38,6 @@
 def outward_block(packed, slot_ids, counts, row_tiles, col_tiles):
     placed = unpack_tiles(packed, slot_ids, counts, row_tiles, col_tiles)
     return placed.transpose(1, 2, 0, 3).reshape(col_tiles * TILE, row_tiles * TILE)
-
-
-def even_odd(width):
-    source = jnp.arange(width)[:, None]
-    place = jnp.arange(width)[None, :]
-    inner = place % TILE
-    wanted = place - inner + 2 * (inner % (TILE // 2)) + inner // (TILE // 2)
-    return (source == wanted).astype(jnp.bfloat16)
-
-
-def unpack_kernel(row_tiles, col_tiles, outward, ids_ref, packed_ref, out_ref, spread):
-    slots = packed_ref.shape[0]
-    pairs = TILE // 2
-    blocks = col_tiles // 8
-    tiles = row_tiles * col_tiles
-    wide = 512
-    tile = lax.broadcasted_iota(jnp.int32, (tiles, slots), 0)
-    select = (tile == ids_ref[...]).astype(jnp.bfloat16)
-
-    def place(step, carry):
-        columns = pl.ds(pl.multiple_of(step * wide, wide), wide)
-        placed = jnp.dot(select, packed_ref[:, columns], preferred_element_type=jnp.float32)
-        for sub in range(wide // 128):
-            for block in range(tiles // 8):
-                start = block * pairs * 8 + (step * (wide // 128) + sub) * 8
-                spread[pl.ds(pl.multiple_of(start, 8), 8), :] = placed[
-                    block * 8 : block * 8 + 8, sub * 128 : sub * 128 + 128
-                ]
-        return carry
-
-    lax.fori_loop(0, TILE * TILE // wide, place, 0)
-    low = lax.broadcasted_iota(jnp.int32, (pairs, 128), 1) < TILE
-
-    def join(left, right):
-        even = jnp.where(low, left, pltpu.roll(right, TILE, 1))
-        odd = jnp.where(low, pltpu.roll(left, TILE, 1), right)
-        return even.astype(jnp.bfloat16), odd.astype(jnp.bfloat16)
-
-    def build(step, carry):
-        def tile_at(row, sub):
-            start = (row * blocks + step // 2) * pairs * 8 + (step % 2) * 4 + sub
-            return spread[pl.ds(start, pairs, stride=8), :]
-
-        if outward:
-            for sub in range(4):
-                for half in range(row_tiles // 2):
-                    parts = join(tile_at(2 * half, sub), tile_at(2 * half + 1, sub))
-                    for odd in range(2):
-                        at = sub * TILE + odd * pairs
-                        out_ref[step, at : at + pairs, half * 128 : half * 128 + 128] = parts[odd]
-        else:
-            for row in range(row_tiles):
-                for half in range(2):
-                    parts = join(tile_at(row, 2 * half), tile_at(row, 2 * half + 1))
-                    for odd in range(2):
-                        at = row * TILE + odd * pairs
-                        out_ref[step, at : at + pairs, half * 128 : half * 128 + 128] = parts[odd]
-        return carry
-
-    lax.fori_loop(0, col_tiles // 4, build, 0)
-
-
-def unpack(packed, ids, row_tiles, col_tiles, outward):
-    groups = col_tiles // 4
-    if outward:
-        shape = (groups, 4 * TILE, row_tiles * TILE)
-    else:
-        shape = (groups, row_tiles * TILE, 4 * TILE)
-    return pl.pallas_call(
-        lambda *refs: unpack_kernel(row_tiles, col_tiles, outward, *refs),
-        out_shape=jax.ShapeDtypeStruct(shape, jnp.bfloat16),
-        in_specs=[pl.BlockSpec(memory_space=pltpu.VMEM)] * 2,
-        out_specs=pl.BlockSpec(memory_space=pltpu.VMEM),
-        scratch_shapes=[pltpu.VMEM((row_tiles * col_tiles * TILE // 2, 128), jnp.float32)],
-        compiler_params=pltpu.CompilerParams(vmem_limit_bytes=32 << 20),
-        cost_estimate=pl.CostEstimate(flops=2 * 10**9, bytes_accessed=6 << 20, transcendentals=0),
-        name="unpack_out" if outward else "unpack_in",
-    )(ids, packed)
 
 
 def gather_features(tokens, norm_gain):
@@ -155,9 +77,15 @@
     return spread_rows(jnp.dot(hidden, down_block, preferred_element_type=jnp.float32))
 
 
+LAG = 2
+WIDE = 512
+
+
 def flow_kernel(
-    n_dp, n_tensor, normed, order, gate_w, up_w, down_w, out,
-    xa, xg, xp, part, pair, chain, hid, acc, tail, tail_in, mixed, back,
+    n_dp, n_tensor, row_tiles, col_tiles,
+    tokens_in, gain, ids, counts, gate_p, up_p, down_p, out,
+    normed, order, packed, gate_t, up_t, down_t, inward_w, down_w,
+    xa, xg, xp, part, pair, chain, hid, acc, tail, tail_in, mixed, back, load_s,
     head_s, head_r, row_s, row_r, pair_s, pair_r, chain_s, chain_r,
     hid_s, hid_r, core_s, core_r, tail_s, tail_r, back_s, back_r,
 ):
@@ -165,7 +93,7 @@
     z, core = me // 2, me % 2
     chips = n_dp // 2
     last = chips - 1
-    groups = gate_w.shape[0]
+    groups = part.shape[0]
     rows, width = xa.shape[1], xa.shape[2]
     other = 1 - core
     buddy = z * 2 + other
@@ -180,7 +108,77 @@
         pl.semaphore_signal(
             barrier, inc=1, device_id=(me, (mt + d) % n_tensor), device_id_type=MESH
         )
+    loads = [
+        pltpu.make_async_copy(source, packed.at[i], load_s.at[i])
+        for i, source in enumerate((gate_p, up_p, down_p))
+    ]
+    for load in loads:
+        load.start()
+
+    wide = tokens_in[...].astype(jnp.float32)
+    meansq = jnp.mean(wide * wide, axis=-1, keepdims=True)
+    normed[...] = (wide * lax.rsqrt(meansq + 1e-05) * gain[...]).astype(jnp.bfloat16)
+    source = lax.broadcasted_iota(jnp.int32, (256, 256), 0)
+    place = lax.broadcasted_iota(jnp.int32, (256, 256), 1)
+    inner = place & (TILE - 1)
+    wanted = place - inner + 2 * (inner & (TILE // 2 - 1)) + (inner >> 5)
+    order[...] = (source == wanted).astype(jnp.bfloat16)
     pl.semaphore_wait(barrier, n_dp + n_tensor - 2)
+
+    pairs = TILE // 2
+    blocks = col_tiles // 8
+    tiles = row_tiles * col_tiles
+    slots = packed.shape[1]
+    low = lax.broadcasted_iota(jnp.int32, (pairs, 128), 1) < TILE
+
+    def place_tiles(which, spread, at):
+        tile = lax.broadcasted_iota(jnp.int32, (tiles, slots), 0)
+        slot = lax.broadcasted_iota(jnp.int32, (tiles, slots), 1)
+        hit = (tile == ids[which : which + 1, :]) & (slot < counts[which : which + 1, :])
+        columns = pl.ds(pl.multiple_of(at * WIDE, WIDE), WIDE)
+        placed = jnp.dot(
+            hit.astype(jnp.bfloat16), packed[which, :, columns], preferred_element_type=jnp.float32
+        )
+        for sub in range(WIDE // 128):
+            for block in range(tiles // 8):
+                start = block * pairs * 8 + (at * (WIDE // 128) + sub) * 8
+                spread[pl.ds(pl.multiple_of(start, 8), 8), :] = placed[
+                    block * 8 : block * 8 + 8, sub * 128 : sub * 128 + 128
+                ]
+
+    def place_all(which, spread):
+        def body(at, carry):
+            place_tiles(which, spread, at)
+            return carry
+
+        lax.fori_loop(0, TILE * TILE // WIDE, body, 0)
+
+    def tile_at(spread, n, row, sub):
+        start = (row * blocks + n // 4) * pairs * 8 + (n % 4) * 2 + sub
+        return spread[pl.ds(start, pairs, stride=8), :]
+
+    def join(left, right):
+        even = jnp.where(low, left, pltpu.roll(right, TILE, 1))
+        odd = jnp.where(low, pltpu.roll(left, TILE, 1), right)
+        return even.astype(jnp.bfloat16), odd.astype(jnp.bfloat16)
+
+    def build_inward(n):
+        for which, spread in enumerate((gate_t, up_t)):
+            for row in range(row_tiles):
+                both = join(tile_at(spread, n, row, 0), tile_at(spread, n, row, 1))
+                for odd in range(2):
+                    at = row * TILE + odd * pairs
+                    inward_w[at : at + pairs, which * 128 : which * 128 + 128] = both[odd]
+
+    def build_down(n):
+        for sub in range(2):
+            for half in range(row_tiles // 2):
+                both = join(
+                    tile_at(down_t, n, 2 * half, sub), tile_at(down_t, n, 2 * half + 1, sub)
+                )
+                for odd in range(2):
+                    at = sub * TILE + odd * pairs
+                    down_w[at : at + pairs, half * 128 : half * 128 + 128] = both[odd]
 
     def send(src, dst, send_sem, recv_sem, dp, tensor):
         return pltpu.make_async_remote_copy(
@@ -201,11 +199,15 @@
     for d in range(1, n_dp):
         head(d).start()
     xa[me] = normed[:, slab(me)]
+    loads[0].wait()
+    place_all(0, gate_t)
     for d in range(1, n_dp):
         head(d).wait_recv()
     for d in range(1, n_tensor):
         row(d).start()
     xg[mt] = xa[...]
+    loads[1].wait()
+    place_all(1, up_t)
     for d in range(1, n_tensor):
         row(d).wait_recv()
     tokens = n_tensor * n_dp * rows
@@ -217,6 +219,7 @@
             preferred_element_type=jnp.float32,
         ).astype(jnp.bfloat16)
     acc[...] = jnp.zeros_like(acc)
+    loads[2].wait()
 
     def pair_copy(n):
         return send(part.at[n, :, other], pair.at[n], pair_s.at[n], pair_r.at[n], buddy, mt)
@@ -239,11 +242,9 @@
         )
 
     def project(n):
-        for which, weight in enumerate((gate_w, up_w)):
-            value = jnp.dot(xp[...], weight[n], preferred_element_type=jnp.float32)
-            part[n, :, :, :, which * 256 : which * 256 + 256] = value.astype(
-                jnp.bfloat16
-            ).reshape(2, 2, quarter, 256)
+        build_inward(n)
+        value = jnp.dot(xp[...], inward_w[...], preferred_element_type=jnp.float32)
+        part[n] = value.astype(jnp.bfloat16).reshape(2, 2, quarter, 256)
         pair_copy(n).start()
 
     def inside(n):
@@ -256,13 +257,13 @@
     farthest = jnp.maximum(z, last - z)
 
     def step(s, carry):
-        @pl.when(inside(s - nearest))
+        @pl.when(inside(s - LAG * nearest))
         def _():
-            pair_copy(s - nearest).wait_recv()
+            pair_copy(s - LAG * nearest).wait_recv()
 
         for h in range(2):
             position = hops[h][0]
-            n = s - position
+            n = s - LAG * position
 
             @pl.when(inside(n))
             def _():
@@ -288,15 +289,15 @@
                 @pl.when(position == last)
                 def _():
                     total = own() + chain[n, h].astype(jnp.float32)
-                    gate = total[:, :256]
-                    value = gate / (1.0 + jnp.exp(-gate)) * total[:, 256:]
+                    gate = total[:, :128]
+                    value = gate / (1.0 + jnp.exp(-gate)) * total[:, 128:]
                     hid[n, h, core] = jnp.dot(
-                        value.astype(jnp.bfloat16), order[...], preferred_element_type=jnp.float32
+                        value.astype(jnp.bfloat16), order[:128, :128], preferred_element_type=jnp.float32
                     ).astype(jnp.bfloat16)
 
         for h in range(2):
             distance = last - hops[h][0]
-            n = s - last - distance
+            n = s - LAG * (last + distance)
 
             @pl.when(inside(n))
             def _():
@@ -314,19 +315,24 @@
         def _():
             project(s + ahead)
 
-        done = s - last - farthest - 1
+        @pl.when(s < TILE * TILE // WIDE)
+        def _():
+            place_tiles(2, down_t, s)
+
+        done = s - LAG * (last + farthest) - 1
 
         @pl.when(inside(done))
         def _():
             for h in range(2):
                 core_copy(done, h).wait_recv()
+            build_down(done)
             acc[...] += jnp.dot(
-                hid[done].reshape(tokens, 256), down_w[done], preferred_element_type=jnp.float32
+                hid[done].reshape(tokens, 128), down_w[...], preferred_element_type=jnp.float32
             )
 
         return carry
 
-    lax.fori_loop(0, groups + 2 * last + 1, step, 0)
+    lax.fori_loop(0, groups + 2 * LAG * last + 1, step, 0)
 
     tail[...] = acc[...].astype(jnp.bfloat16).reshape(tail.shape)
 
@@ -378,62 +384,71 @@
         out[:, p * width : p * width + width] = back[p]
 
 
-def flow(normed, order, gate_w, up_w, down_w, n_dp, n_tensor):
-    groups, width, _ = gate_w.shape
-    rows = normed.shape[0]
-    tokens = rows * n_dp * n_tensor
-    quarter = tokens // 4
+def flow(tokens, gain, ids, counts, gate_p, up_p, down_p, n_dp, n_tensor, row_tiles, col_tiles):
+    groups = col_tiles // 2
+    width = row_tiles * TILE
+    rows = tokens.shape[0]
+    total = rows * n_dp * n_tensor
+    quarter = total // 4
+    tiles = row_tiles * col_tiles
     half = jnp.bfloat16
     dma = pltpu.SemaphoreType.DMA
+    vmem = pl.BlockSpec(memory_space=pltpu.VMEM)
     return pl.pallas_call(
-        lambda *refs: flow_kernel(n_dp, n_tensor, *refs),
-        out_shape=jax.ShapeDtypeStruct(normed.shape, half),
-        in_specs=[pl.BlockSpec(memory_space=pltpu.VMEM)] * 5,
-        out_specs=pl.BlockSpec(memory_space=pltpu.VMEM),
+        lambda *refs: flow_kernel(n_dp, n_tensor, row_tiles, col_tiles, *refs),
+        out_shape=jax.ShapeDtypeStruct(tokens.shape, half),
+        in_specs=[vmem] * 4 + [pl.BlockSpec(memory_space=pl.ANY)] * 3,
+        out_specs=vmem,
         scratch_shapes=[
+            pltpu.VMEM(tokens.shape, half),
+            pltpu.VMEM((256, 256), half),
+            pltpu.VMEM((3,) + gate_p.shape, half),
+            pltpu.VMEM((tiles * TILE // 2, 128), jnp.float32),
+            pltpu.VMEM((tiles * TILE // 2, 128), jnp.float32),
+            pltpu.VMEM((tiles * TILE // 2, 128), jnp.float32),
+            pltpu.VMEM((width, 256), half),
+            pltpu.VMEM((128, width), half),
             pltpu.VMEM((n_dp, rows, width), half),
             pltpu.VMEM((n_tensor, n_dp, rows, width), half),
-            pltpu.VMEM((tokens, width), half),
-            pltpu.VMEM((groups, 2, 2, quarter, 512), half),
-            pltpu.VMEM((groups, 2, quarter, 512), half),
-            pltpu.VMEM((groups, 2, quarter, 512), half),
+            pltpu.VMEM((total, width), half),
             pltpu.VMEM((groups, 2, 2, quarter, 256), half),
-            pltpu.VMEM((tokens, width), jnp.float32),
+            pltpu.VMEM((groups, 2, quarter, 256), half),
+            pltpu.VMEM((groups, 2, quarter, 256), half),
+            pltpu.VMEM((groups, 2, 2, quarter, 128), half),
+            pltpu.VMEM((total, width), jnp.float32),
             pltpu.VMEM((n_tensor, n_dp * rows, width), half),
             pltpu.VMEM((n_tensor, n_dp * rows, width), half),
             pltpu.VMEM((n_dp, rows, width), half),
             pltpu.VMEM((n_dp, rows, width), half),
+            dma((3,)),
             dma((n_dp,)), dma((n_dp,)), dma((n_tensor,)), dma((n_tensor,)),
             dma((groups,)), dma((groups,)), dma((groups, 2)), dma((groups, 2)),
             dma((groups, 2)), dma((groups, 2)), dma((groups, 2)), dma((groups, 2)),
             dma((n_tensor,)), dma((n_tensor,)), dma((n_dp,)), dma((n_dp,)),
         ],
         compiler_params=pltpu.CompilerParams(
-            collective_id=0, has_side_effects=True, vmem_limit_bytes=56 << 20
+            collective_id=0, has_side_effects=True, vmem_limit_bytes=60 << 20
         ),
         cost_estimate=pl.CostEstimate(
-            flops=6 * 10**9, bytes_accessed=12 << 20, transcendentals=10**6
+            flops=9 * 10**9, bytes_accessed=6 << 20, transcendentals=10**6
         ),
         name="flow",
-    )(normed, order, gate_w, up_w, down_w)
+    )(tokens, gain, ids, counts, gate_p, up_p, down_p)
 
 
 def local(tokens, norm_gain, gate_tiles, up_tiles, down_tiles, tile_ids, tile_counts):
     n_dp, n_tensor = lax.axis_size("dp"), lax.axis_size("tensor")
     row_tiles = D // (TILE * n_dp)
     col_tiles = FF // (TILE * n_tensor)
-    if col_tiles % 8 != 0 or row_tiles % 4 != 0 or n_tensor != 4 or n_dp % 2 != 0:
+    if col_tiles % 8 != 0 or row_tiles % 4 != 0 or n_tensor != 4 or n_dp != 8:
         return local_plain(
             tokens, norm_gain, gate_tiles, up_tiles, down_tiles, tile_ids, tile_counts
         )
-    slots = tile_ids.shape[-1]
-    kept = jnp.arange(slots)[None, :] < tile_counts[0, 0][:, None]
-    ids = jnp.where(kept, tile_ids[0, 0], -1)
-    gate_w = unpack(gate_tiles[0, 0], ids[0:1], row_tiles, col_tiles, False)
-    up_w = unpack(up_tiles[0, 0], ids[1:2], row_tiles, col_tiles, False)
-    down_w = unpack(down_tiles[0, 0], ids[2:3], row_tiles, col_tiles, True)
-    normed = normalize(tokens, norm_gain)
-    return flow(normed, even_odd(256), gate_w, up_w, down_w, n_dp, n_tensor)
+    return flow(
+        tokens, norm_gain[None, :], tile_ids[0, 0], tile_counts[0, 0][:, None],
+        gate_tiles[0, 0], up_tiles[0, 0], down_tiles[0, 0],
+        n_dp, n_tensor, row_tiles, col_tiles,
+    )
 
 
 def solution(mesh):

time: 150 us -> 119 us (0.79)
  Pallas kernels: 137 us -> 114 us
  local copies, waits for them, and re-layouts: 8.7 us -> 4.17 us
  other arithmetic: 4.17 us -> 0 us
    pallas_call x4 -> x1, Pallas kernels: 137 us -> 114 us  [flow(): pl.pallas_call(lambda *refs: flow_kernel(n_dp, n_tensor, row_tiles, col_t...]
    unnamed x13 -> x2, local copies, waits for them, and re-layouts: 8.7 us -> 2.85 us
    convert_element_type x2 -> x0, other arithmetic: 2.34 us -> none  [the longest x1 1.66 us: normalize(): return (wide * lax.rsqrt(meansq + 1e-05) * norm_gain).astype(jnp.bfloat16)]
where the time goes in v2:
time: 119 us; the launch traced here: 118 us
  Pallas kernels  114 us (96%)
  local copies, waits for them, and re-layouts  4.17 us (4%)
    pallas_call x1, Pallas kernels, flow(): pl.pallas_call(lambda *refs: flow_kernel(n_dp, n_tensor, row_tiles, col_t...  114 us
    unnamed x2, local copies, waits for them, and re-layouts  2.85 us

profile of v2, /device:TPU:0, one launch (start us, length us, event | category | flops | bytes accessed | tf_op | source)
XLA Modules:
  0.0 118.4 jit_solution(16927585798270194827)
XLA Ops:
  0.0 1.3 %copy.8.refs_3_ = s32[3,1]{1,0:T(4,128)} copy(s32[3,1]{0,1:T(1,128)} %bitcast.9) | data formatting | bytes 24 | tf_op jit(solution)/shard_map/broadcast_in_dim;squeeze | solution.py:448
  1.3 1.3 %copy.11 = s32[1,1,3,256]{3,2,1,0:T(4,128)} copy(s32[1,1,3,256]{3,1,2,0:T(1,128)} %param.12) | data formatting | bytes 6144
  2.6 114.2 %flow.1 = bf16[16,4096]{1,0:T(8,128)(2,1)} custom-call(bf16[16,4096]{1,0:T(8,128)(2,1)} %refs_0_.1, f32[1,4096]{1,0:T(1,128)} %bitcast.13, s32[3,256]{1,0:T(4,128)} %bitcast.8, s32[3,1]{1,0:T(4,128)} %copy.8.refs_3_, bf16[256,4096]{1,0:T(8,128)(2,1)} %bitcast.10, bf16[256,4096]{1,0:T(8,128)(2,1)} %bitcast.11, bf16[256,4096]{1,0:T(8,128)(2,1)} %bitcast.12), custom_call_target="tpu_custom_call" | custom-call | flops 8999999488 | bytes 6291456 | tf_op jit(solution)/shard_map/flow/pallas_call | solution.py:397
  116.8 1.6 %copy.13 = bf16[16,4096]{1,0:T(8,128)(2,1)} copy(bf16[16,4096]{1,0:T(8,128)(2,1)} %flow.1) | data formatting | bytes 262144

commit v3 on v2

--- a/solution.py
+++ b/solution.py
@@ -117,7 +117,7 @@
 
     wide = tokens_in[...].astype(jnp.float32)
     meansq = jnp.mean(wide * wide, axis=-1, keepdims=True)
-    normed[...] = (wide * lax.rsqrt(meansq + 1e-05) * gain[...]).astype(jnp.bfloat16)
+    normed[...] = (wide * lax.rsqrt(meansq + 1e-05) * gain[...].reshape(1, D)).astype(jnp.bfloat16)
     source = lax.broadcasted_iota(jnp.int32, (256, 256), 0)
     place = lax.broadcasted_iota(jnp.int32, (256, 256), 1)
     inner = place & (TILE - 1)
@@ -134,7 +134,7 @@
     def place_tiles(which, spread, at):
         tile = lax.broadcasted_iota(jnp.int32, (tiles, slots), 0)
         slot = lax.broadcasted_iota(jnp.int32, (tiles, slots), 1)
-        hit = (tile == ids[which : which + 1, :]) & (slot < counts[which : which + 1, :])
+        hit = (tile == ids[which]) & (slot < counts[0, 0, which])
         columns = pl.ds(pl.multiple_of(at * WIDE, WIDE), WIDE)
         placed = jnp.dot(
             hit.astype(jnp.bfloat16), packed[which, :, columns], preferred_element_type=jnp.float32
@@ -170,7 +170,7 @@
                     at = row * TILE + odd * pairs
                     inward_w[at : at + pairs, which * 128 : which * 128 + 128] = both[odd]
 
-    def build_down(n):
+    def build_down(n, slot):
         for sub in range(2):
             for half in range(row_tiles // 2):
                 both = join(
@@ -178,7 +178,7 @@
                 )
                 for odd in range(2):
                     at = sub * TILE + odd * pairs
-                    down_w[at : at + pairs, half * 128 : half * 128 + 128] = both[odd]
+                    down_w[slot, at : at + pairs, half * 128 : half * 128 + 128] = both[odd]
 
     def send(src, dst, send_sem, recv_sem, dp, tensor):
         return pltpu.make_async_remote_copy(
@@ -325,10 +325,16 @@
         def _():
             for h in range(2):
                 core_copy(done, h).wait_recv()
-            build_down(done)
-            acc[...] += jnp.dot(
-                hid[done].reshape(tokens, 128), down_w[...], preferred_element_type=jnp.float32
-            )
+            build_down(done, done % 2)
+
+            @pl.when(done % 2 == 1)
+            def _():
+                both = jnp.concatenate(
+                    [hid[done - 1].reshape(tokens, 128), hid[done].reshape(tokens, 128)], axis=1
+                )
+                acc[...] += jnp.dot(
+                    both, down_w[...].reshape(256, width), preferred_element_type=jnp.float32
+                )
 
         return carry
 
@@ -397,7 +403,7 @@
     return pl.pallas_call(
         lambda *refs: flow_kernel(n_dp, n_tensor, row_tiles, col_tiles, *refs),
         out_shape=jax.ShapeDtypeStruct(tokens.shape, half),
-        in_specs=[vmem] * 4 + [pl.BlockSpec(memory_space=pl.ANY)] * 3,
+        in_specs=[vmem] * 3 + [pl.BlockSpec(memory_space=pltpu.SMEM)] + [pl.BlockSpec(memory_space=pl.ANY)] * 3,
         out_specs=vmem,
         scratch_shapes=[
             pltpu.VMEM(tokens.shape, half),
@@ -407,7 +413,7 @@
             pltpu.VMEM((tiles * TILE // 2, 128), jnp.float32),
             pltpu.VMEM((tiles * TILE // 2, 128), jnp.float32),
             pltpu.VMEM((width, 256), half),
-            pltpu.VMEM((128, width), half),
+            pltpu.VMEM((2, 128, width), half),
             pltpu.VMEM((n_dp, rows, width), half),
             pltpu.VMEM((n_tensor, n_dp, rows, width), half),
             pltpu.VMEM((total, width), half),
@@ -445,7 +451,7 @@
             tokens, norm_gain, gate_tiles, up_tiles, down_tiles, tile_ids, tile_counts
         )
     return flow(
-        tokens, norm_gain[None, :], tile_ids[0, 0], tile_counts[0, 0][:, None],
+        tokens, norm_gain, tile_ids[0, 0][:, None, :], tile_counts,
         gate_tiles[0, 0], up_tiles[0, 0], down_tiles[0, 0],
         n_dp, n_tensor, row_tiles, col_tiles,
     )

time: 119 us -> 115 us (0.966)
  local copies, waits for them, and re-layouts: 4.17 us -> 1.57 us
    another operation x1 -> x0, local copies, waits for them, and re-layouts: 1.32 us -> none  [local(): tile_counts[0, 0][:, None]]
    unnamed x2 -> x1, local copies, waits for them, and re-layouts: 2.85 us -> 1.57 us
where the time goes in v3:
time: 115 us
  Pallas kernels  114 us (99%)
  local copies, waits for them, and re-layouts  1.57 us (1%)
    pallas_call x1, Pallas kernels, flow(): pl.pallas_call(lambda *refs: flow_kernel(n_dp, n_tensor, row_tiles, col_t...  114 us

profile of v3, /device:TPU:0, one launch (start us, length us, event | category | flops | bytes accessed | tf_op | source)
XLA Modules:
  0.0 115.3 jit_solution(8255899151215534170)
XLA Ops:
  0.0 113.7 %flow.1 = bf16[16,4096]{1,0:T(8,128)(2,1)} custom-call(bf16[16,4096]{1,0:T(8,128)(2,1)} %refs_0_.1, f32[4096]{0:T(1024)} %refs_1_.1, s32[3,1,256]{2,1,0:T(1,128)} %bitcast.7, s32[1,1,3]{2,1,0:T(1,128)} %refs_3_.1, bf16[256,4096]{1,0:T(8,128)(2,1)} %bitcast.4, bf16[256,4096]{1,0:T(8,128)(2,1)} %bitcast.5, bf16[256,4096]{1,0:T(8,128)(2,1)} %bitcast.6), custom_call_target="tpu_custom_call" | custom-call | flops 8999999488 | bytes 6291456 | tf_op jit(solution)/shard_map/flow/pallas_call | solution.py:403
  113.7 1.6 %copy.9 = bf16[16,4096]{1,0:T(8,128)(2,1)} copy(bf16[16,4096]{1,0:T(8,128)(2,1)} %flow.1) | data formatting | bytes 262144

commit v4 on v3

--- a/solution.py
+++ b/solution.py
@@ -208,6 +208,9 @@
     xg[mt] = xa[...]
     loads[1].wait()
     place_all(1, up_t)
+    loads[2].wait()
+    place_all(2, down_t)
+    acc[...] = jnp.zeros_like(acc)
     for d in range(1, n_tensor):
         row(d).wait_recv()
     tokens = n_tensor * n_dp * rows
@@ -218,8 +221,6 @@
             order[...],
             preferred_element_type=jnp.float32,
         ).astype(jnp.bfloat16)
-    acc[...] = jnp.zeros_like(acc)
-    loads[2].wait()
 
     def pair_copy(n):
         return send(part.at[n, :, other], pair.at[n], pair_s.at[n], pair_r.at[n], buddy, mt)
@@ -314,10 +315,6 @@
         @pl.when(s + ahead < groups)
         def _():
             project(s + ahead)
-
-        @pl.when(s < TILE * TILE // WIDE)
-        def _():
-            place_tiles(2, down_t, s)
 
         done = s - LAG * (last + farthest) - 1
 
@@ -353,6 +350,27 @@
     for d in range(1, n_tensor):
         tail_copy(d).start()
     tail_in[mt] = tail[mt]
+
+    def drain(n, carry):
+        pair_copy(n).wait_send()
+        for h in range(2):
+            core_copy(n, h).wait_send()
+
+            @pl.when(hops[h][0] < last)
+            def _():
+                chain_copy(n, h).wait_send()
+
+            @pl.when(last - hops[h][0] < last)
+            def _():
+                hid_copy(n, h).wait_send()
+
+        return carry
+
+    lax.fori_loop(0, groups, drain, 0)
+    for d in range(1, n_dp):
+        head(d).wait_send()
+    for d in range(1, n_tensor):
+        row(d).wait_send()
     for d in range(1, n_tensor):
         tail_copy(d).wait_recv()
     total = tail_in[0].astype(jnp.float32)
@@ -363,28 +381,10 @@
         back_copy(d).start()
     back[me] = mixed[me]
 
-    def drain(n, carry):
-        pair_copy(n).wait_send()
-        for h in range(2):
-            core_copy(n, h).wait_send()
-
-            @pl.when(hops[h][0] < last)
-            def _():
-                chain_copy(n, h).wait_send()
-
-            @pl.when(last - hops[h][0] < last)
-            def _():
-                hid_copy(n, h).wait_send()
-
-        return carry
-
-    lax.fori_loop(0, groups, drain, 0)
-    for d in range(1, n_dp):
-        head(d).wait_send()
+    for d in range(1, n_dp):
         back_copy(d).wait_recv()
         back_copy(d).wait_send()
     for d in range(1, n_tensor):
-        row(d).wait_send()
         tail_copy(d).wait_send()
     for p in range(n_dp):
         out[:, p * width : p * width + width] = back[p]

time: 115 us -> 115 us (level)
  no operation moved by 1% of the time
where the time goes in v4:
time: 115 us
  Pallas kernels  113 us (98%)
  local copies, waits for them, and re-layouts  1.57 us (1%)
    pallas_call x1, Pallas kernels, flow(): pl.pallas_call(lambda *refs: flow_kernel(n_dp, n_tensor, row_tiles, col_t...  113 us

profile of v4, /device:TPU:0, one launch (start us, length us, event | category | flops | bytes accessed | tf_op | source)
XLA Modules:
  0.0 115.1 jit_solution(14297418752600726229)
XLA Ops:
  0.0 113.5 %flow.1 = bf16[16,4096]{1,0:T(8,128)(2,1)} custom-call(bf16[16,4096]{1,0:T(8,128)(2,1)} %refs_0_.1, f32[4096]{0:T(1024)} %refs_1_.1, s32[3,1,256]{2,1,0:T(1,128)} %bitcast.7, s32[1,1,3]{2,1,0:T(1,128)} %refs_3_.1, bf16[256,4096]{1,0:T(8,128)(2,1)} %bitcast.4, bf16[256,4096]{1,0:T(8,128)(2,1)} %bitcast.5, bf16[256,4096]{1,0:T(8,128)(2,1)} %bitcast.6), custom_call_target="tpu_custom_call" | custom-call | flops 8999999488 | bytes 6291456 | tf_op jit(solution)/shard_map/flow/pallas_call | solution.py:403
  113.5 1.6 %copy.9 = bf16[16,4096]{1,0:T(8,128)(2,1)} copy(bf16[16,4096]{1,0:T(8,128)(2,1)} %flow.1) | data formatting | bytes 262144

commit v5 on v4

--- a/solution.py
+++ b/solution.py
@@ -258,6 +258,22 @@
     farthest = jnp.maximum(z, last - z)
 
     def step(s, carry):
+        for h in range(2):
+            distance = last - hops[h][0]
+            n = s - LAG * last - 1 - distance
+
+            @pl.when(inside(n))
+            def _():
+                @pl.when(distance > 0)
+                def _():
+                    hid_copy(n, h).wait_recv()
+
+                @pl.when(distance < last)
+                def _():
+                    hid_copy(n, h).start()
+
+                core_copy(n, h).start()
+
         @pl.when(inside(s - LAG * nearest))
         def _():
             pair_copy(s - LAG * nearest).wait_recv()
@@ -296,27 +312,11 @@
                         value.astype(jnp.bfloat16), order[:128, :128], preferred_element_type=jnp.float32
                     ).astype(jnp.bfloat16)
 
-        for h in range(2):
-            distance = last - hops[h][0]
-            n = s - LAG * (last + distance)
-
-            @pl.when(inside(n))
-            def _():
-                @pl.when(distance > 0)
-                def _():
-                    hid_copy(n, h).wait_recv()
-
-                @pl.when(distance < last)
-                def _():
-                    hid_copy(n, h).start()
-
-                core_copy(n, h).start()
-
         @pl.when(s + ahead < groups)
         def _():
             project(s + ahead)
 
-        done = s - LAG * (last + farthest) - 1
+        done = s - LAG * last - farthest - 2
 
         @pl.when(inside(done))
         def _():
@@ -335,7 +335,7 @@
 
         return carry
 
-    lax.fori_loop(0, groups + 2 * LAG * last + 1, step, 0)
+    lax.fori_loop(0, groups + LAG * last + last + 2, step, 0)
 
     tail[...] = acc[...].astype(jnp.bfloat16).reshape(tail.shape)
 

time: 115 us -> 132 us (1.15)
  Pallas kernels: 113 us -> 131 us
    pallas_call x1, Pallas kernels: 113 us -> 131 us  [flow(): pl.pallas_call(lambda *refs: flow_kernel(n_dp, n_tensor, row_tiles, col_t...]
where the time goes in v5:
time: 132 us
  Pallas kernels  131 us (99%)
  local copies, waits for them, and re-layouts  1.57 us (1%)
    pallas_call x1, Pallas kernels, flow(): pl.pallas_call(lambda *refs: flow_kernel(n_dp, n_tensor, row_tiles, col_t...  131 us

profile of v5, /device:TPU:0, one launch (start us, length us, event | category | flops | bytes accessed | tf_op | source)
XLA Modules:
  0.0 132.3 jit_solution(8808746898196856841)
XLA Ops:
  0.0 130.8 %flow.1 = bf16[16,4096]{1,0:T(8,128)(2,1)} custom-call(bf16[16,4096]{1,0:T(8,128)(2,1)} %refs_0_.1, f32[4096]{0:T(1024)} %refs_1_.1, s32[3,1,256]{2,1,0:T(1,128)} %bitcast.7, s32[1,1,3]{2,1,0:T(1,128)} %refs_3_.1, bf16[256,4096]{1,0:T(8,128)(2,1)} %bitcast.4, bf16[256,4096]{1,0:T(8,128)(2,1)} %bitcast.5, bf16[256,4096]{1,0:T(8,128)(2,1)} %bitcast.6), custom_call_target="tpu_custom_call" | custom-call | flops 8999999488 | bytes 6291456 | tf_op jit(solution)/shard_map/flow/pallas_call | solution.py:403
  130.8 1.6 %copy.9 = bf16[16,4096]{1,0:T(8,128)(2,1)} copy(bf16[16,4096]{1,0:T(8,128)(2,1)} %flow.1) | data formatting | bytes 262144

commit v6 on v4

--- a/solution.py
+++ b/solution.py
@@ -77,7 +77,7 @@
     return spread_rows(jnp.dot(hidden, down_block, preferred_element_type=jnp.float32))
 
 
-LAG = 2
+LAG = 3
 WIDE = 512
 
 

time: 115 us -> 113 us (0.983)
  Pallas kernels: 113 us -> 111 us
    pallas_call x1, Pallas kernels: 113 us -> 111 us  [flow(): pl.pallas_call(lambda *refs: flow_kernel(n_dp, n_tensor, row_tiles, col_t...]
where the time goes in v6:
time: 113 us
  Pallas kernels  111 us (98%)
  local copies, waits for them, and re-layouts  1.57 us (1%)
    pallas_call x1, Pallas kernels, flow(): pl.pallas_call(lambda *refs: flow_kernel(n_dp, n_tensor, row_tiles, col_t...  111 us

profile of v6, /device:TPU:0, one launch (start us, length us, event | category | flops | bytes accessed | tf_op | source)
XLA Modules:
  0.0 112.5 jit_solution(82984403864929673)
XLA Ops:
  0.0 111.0 %flow.1 = bf16[16,4096]{1,0:T(8,128)(2,1)} custom-call(bf16[16,4096]{1,0:T(8,128)(2,1)} %refs_0_.1, f32[4096]{0:T(1024)} %refs_1_.1, s32[3,1,256]{2,1,0:T(1,128)} %bitcast.7, s32[1,1,3]{2,1,0:T(1,128)} %refs_3_.1, bf16[256,4096]{1,0:T(8,128)(2,1)} %bitcast.4, bf16[256,4096]{1,0:T(8,128)(2,1)} %bitcast.5, bf16[256,4096]{1,0:T(8,128)(2,1)} %bitcast.6), custom_call_target="tpu_custom_call" | custom-call | flops 8999999488 | bytes 6291456 | tf_op jit(solution)/shard_map/flow/pallas_call | solution.py:403
  111.0 1.6 %copy.9 = bf16[16,4096]{1,0:T(8,128)(2,1)} copy(bf16[16,4096]{1,0:T(8,128)(2,1)} %flow.1) | data formatting | bytes 262144
